TPU v7x, 128 devices: a whole 4x4x4 slice. The times are simulated.
128 devices in a mesh: ctx: 32 (over x, z_lo, y), head: 4 (over z_hi, core).
Axes of the slice: x: 4, y: 4, z: 4 (z_hi: 2, z_lo: 2; z = z_hi * 2 + z_lo), core: 2. Of those that a mesh axis runs over, the one named last changes fastest.
Arguments:
- queries: bfloat16 [1024, 128, 128], P('ctx', 'head'), may hold values from -60 to 60
- cache_keys: bfloat16 [40960, 8, 128], P('ctx', 'head'), may hold values from -9 to 9
- cache_values: bfloat16 [40960, 8, 128], P('ctx', 'head'), may hold values from -6 to 6
- new_keys: bfloat16 [1024, 8, 128], P('ctx', 'head'), may hold values from -6 to 6
- new_values: bfloat16 [1024, 8, 128], P('ctx', 'head'), may hold values from -6 to 6
- lengths: int32 [32], P('ctx'), may hold values from 2 to 1280
- span_offset: int32 [], replicated, may hold values from 0 to 1023
Outputs:
- attended: bfloat16 [1024, 128, 128], P(('ctx', 'head'))
All inputs are finite; a program needn't handle non-finite values.
Results may differ from a plain program's by a relative error of at most 0.0056.
Values may be sent and summed in bfloat16 or wider, within the bound.
No kernel may reach another device: no remote copies, remote signals or barrier semaphores. Data moves between devices by JAX's collectives and lax.ppermute only.
A program may use at most 128 MiB of HBM per device.

v0:
```python
import jax
import jax.numpy as jnp
from jax import lax
from jax.sharding import PartitionSpec as P


def passed_along(block, axis, distance):
    devices = range(lax.axis_size(axis))
    route = [((i - distance) % len(devices), i) for i in devices]
    return lax.ppermute(block, axis, route)


def block_partial(queries, key_rows, value_rows, cache_length, query_start, key_start, offset):
    query_rows, head_count, head_width = queries.shape
    kv_heads = key_rows.shape[1]
    group_size = head_count // kv_heads
    total_keys = key_rows.shape[0]
    cache_rows = total_keys - query_rows
    grouped = queries.reshape(query_rows, kv_heads, group_size, head_width)
    scores = jnp.einsum(
        "rkgd,ckd->rkgc", grouped, key_rows, preferred_element_type=jnp.float32
    ) * head_width ** (-0.5)
    key_slots = lax.broadcasted_iota(jnp.int32, (query_rows, total_keys), 1)
    row_limit = query_start + offset + lax.broadcasted_iota(jnp.int32, (query_rows, total_keys), 0)
    visible = jnp.where(
        key_slots < cache_rows,
        key_slots < cache_length,
        key_start + key_slots - cache_rows <= row_limit,
    )
    visible = visible[:, None, None, :]
    masked = jnp.where(visible, scores, jnp.float32(-1e30))
    maxima = jnp.max(masked, axis=-1)
    probabilities = jnp.where(visible, jnp.exp(masked - maxima[..., None]), jnp.float32(0.0))
    totals = jnp.sum(probabilities, axis=-1)
    weighted = jnp.einsum(
        "rkgc,ckd->rkgd",
        probabilities.astype(jnp.bfloat16),
        value_rows,
        preferred_element_type=jnp.float32,
    )
    partial_out = (weighted / totals[..., None]).astype(jnp.bfloat16)
    return (
        partial_out.reshape(query_rows, head_count, head_width),
        maxima.reshape(query_rows, head_count),
        totals.reshape(query_rows, head_count),
    )


def record(buffers, result, anchor, head_start):
    updated = []
    for buffer, piece in zip(buffers, result):
        starts = (anchor, 0, head_start) + (0,) * (buffer.ndim - 3)
        updated.append(lax.dynamic_update_slice(buffer, piece[None], starts))
    return tuple(updated)


def combine(partials, maxima, totals):
    overall = jnp.max(maxima, axis=0)
    weights = totals * jnp.exp(maxima - overall)
    summed = jnp.sum(weights[..., None] * partials, axis=0)
    return (summed / jnp.sum(weights, axis=0)[..., None]).astype(jnp.bfloat16)


def per_device(queries, cache_keys, cache_values, new_keys, new_values, lengths, span_offset):
    query_rows, head_count, head_width = queries.shape
    local_keys = jnp.concatenate([cache_keys, new_keys], 0)
    local_values = jnp.concatenate([cache_values, new_values], 0)
    shard_count = lax.axis_size("ctx")
    own_index = lax.axis_index("ctx")
    own_start = own_index * query_rows
    cache_length = lengths[0]
    empty_parts = (
        jnp.zeros((shard_count, query_rows, head_count, head_width), jnp.bfloat16),
        jnp.zeros((shard_count, query_rows, head_count), jnp.float32),
        jnp.zeros((shard_count, query_rows, head_count), jnp.float32),
    )
    opening = block_partial(
        queries, local_keys, local_values, cache_length, own_start, own_start, span_offset
    )
    buffers = record(empty_parts, opening, own_index, 0)

    def advance(step_index, state_now):
        visiting, buffers = state_now
        visiting = passed_along(visiting, "ctx", 1)
        anchor = (own_index - step_index) % shard_count
        result = block_partial(
            visiting,
            local_keys,
            local_values,
            cache_length,
            anchor * query_rows,
            own_start,
            span_offset,
        )
        return (visiting, record(buffers, result, anchor, 0))

    buffers = lax.fori_loop(1, shard_count, advance, (queries, buffers))[1]
    partials = lax.all_to_all(
        lax.all_to_all(buffers[0], "ctx", split_axis=0, concat_axis=0, tiled=True),
        "head",
        split_axis=1,
        concat_axis=2,
        tiled=True,
    )
    statistics = (
        lax.all_to_all(
            lax.all_to_all(buffers[1], "ctx", split_axis=0, concat_axis=0, tiled=True),
            "head",
            split_axis=1,
            concat_axis=2,
            tiled=True,
        ),
        lax.all_to_all(
            lax.all_to_all(buffers[2], "ctx", split_axis=0, concat_axis=0, tiled=True),
            "head",
            split_axis=1,
            concat_axis=2,
            tiled=True,
        ),
    )
    return combine(partials, statistics[0], statistics[1])


def solution(mesh):
    return jax.shard_map(
        per_device,
        mesh=mesh,
        in_specs=(
            P("ctx", "head", None),
            P("ctx", "head", None),
            P("ctx", "head", None),
            P("ctx", "head", None),
            P("ctx", "head", None),
            P("ctx"),
            P(),
        ),
        out_specs=P(("ctx", "head"), None, None),
        check_vma=False,
    )
```

profile of v0, /device:TPU:24, one launch (start us, length us, event | category | flops | bytes accessed | tf_op | source)
XLA Modules:
  0.0 872.8 jit_solution(2491243037605450320)
XLA Ops:
  16.5 503.8 %while.21 = (s32[]{:T(128)}, bf16[32,32,128]{2,0,1:T(8,128)(2,1)S(1)}, bf16[32,32,32,128]{3,2,1,0:T(8,128)(2,1)}, f32[32,32,32]{1,2,0:T(8,128)S(1)}, f32[32,32,3...) while((s32[]{:T(128)}, ...), condition=%wide.region_5.6_spmd, body=%wide.region_2.5_spmd.sunk | while | flops 705680512 | bytes 20881400 | solution.py:97
  166.6 9.1 %collective-permute-done = bf16[32,32,128]{2,0,1:T(8,128)(2,1)S(1)} collective-permute-done((bf16[32,32,128]{2,0,1:T(8,128)(2,1)S(1)}, bf16[32,32,128]{2,0,1:T(8,128)(2,1)S(1)}, u32[]{:S(2)}, u32[]{:S(2)}) %collective-permute-start) | collective-permute-done | bytes 262176 | tf_op jit(solution)/shard_map/while/body/eval_jaxpr/ppermute | solution.py:10
  182.8 9.1 %collective-permute-done = bf16[32,32,128]{2,0,1:T(8,128)(2,1)S(1)} collective-permute-done((bf16[32,32,128]{2,0,1:T(8,128)(2,1)S(1)}, bf16[32,32,128]{2,0,1:T(8,128)(2,1)S(1)}, u32[]{:S(2)}, u32[]{:S(2)}) %collective-permute-start) | collective-permute-done | bytes 262176 | tf_op jit(solution)/shard_map/while/body/eval_jaxpr/ppermute | solution.py:10
  199.0 9.8 %collective-permute-done = bf16[32,32,128]{2,0,1:T(8,128)(2,1)S(1)} collective-permute-done((bf16[32,32,128]{2,0,1:T(8,128)(2,1)S(1)}, bf16[32,32,128]{2,0,1:T(8,128)(2,1)S(1)}, u32[]{:S(2)}, u32[]{:S(2)}) %collective-permute-start) | collective-permute-done | bytes 262176 | tf_op jit(solution)/shard_map/while/body/eval_jaxpr/ppermute | solution.py:10
  215.9 11.4 %collective-permute-done = bf16[32,32,128]{2,0,1:T(8,128)(2,1)S(1)} collective-permute-done((bf16[32,32,128]{2,0,1:T(8,128)(2,1)S(1)}, bf16[32,32,128]{2,0,1:T(8,128)(2,1)S(1)}, u32[]{:S(2)}, u32[]{:S(2)}) %collective-permute-start) | collective-permute-done | bytes 262176 | tf_op jit(solution)/shard_map/while/body/eval_jaxpr/ppermute | solution.py:10
  234.4 12.5 %collective-permute-done = bf16[32,32,128]{2,0,1:T(8,128)(2,1)S(1)} collective-permute-done((bf16[32,32,128]{2,0,1:T(8,128)(2,1)S(1)}, bf16[32,32,128]{2,0,1:T(8,128)(2,1)S(1)}, u32[]{:S(2)}, u32[]{:S(2)}) %collective-permute-start) | collective-permute-done | bytes 262176 | tf_op jit(solution)/shard_map/while/body/eval_jaxpr/ppermute | solution.py:10
  254.0 11.2 %collective-permute-done = bf16[32,32,128]{2,0,1:T(8,128)(2,1)S(1)} collective-permute-done((bf16[32,32,128]{2,0,1:T(8,128)(2,1)S(1)}, bf16[32,32,128]{2,0,1:T(8,128)(2,1)S(1)}, u32[]{:S(2)}, u32[]{:S(2)}) %collective-permute-start) | collective-permute-done | bytes 262176 | tf_op jit(solution)/shard_map/while/body/eval_jaxpr/ppermute | solution.py:10
  272.3 10.3 %collective-permute-done = bf16[32,32,128]{2,0,1:T(8,128)(2,1)S(1)} collective-permute-done((bf16[32,32,128]{2,0,1:T(8,128)(2,1)S(1)}, bf16[32,32,128]{2,0,1:T(8,128)(2,1)S(1)}, u32[]{:S(2)}, u32[]{:S(2)}) %collective-permute-start) | collective-permute-done | bytes 262176 | tf_op jit(solution)/shard_map/while/body/eval_jaxpr/ppermute | solution.py:10
  336.5 9.1 %collective-permute-done = bf16[32,32,128]{2,0,1:T(8,128)(2,1)S(1)} collective-permute-done((bf16[32,32,128]{2,0,1:T(8,128)(2,1)S(1)}, bf16[32,32,128]{2,0,1:T(8,128)(2,1)S(1)}, u32[]{:S(2)}, u32[]{:S(2)}) %collective-permute-start) | collective-permute-done | bytes 262176 | tf_op jit(solution)/shard_map/while/body/eval_jaxpr/ppermute | solution.py:10
  352.6 9.1 %collective-permute-done = bf16[32,32,128]{2,0,1:T(8,128)(2,1)S(1)} collective-permute-done((bf16[32,32,128]{2,0,1:T(8,128)(2,1)S(1)}, bf16[32,32,128]{2,0,1:T(8,128)(2,1)S(1)}, u32[]{:S(2)}, u32[]{:S(2)}) %collective-permute-start) | collective-permute-done | bytes 262176 | tf_op jit(solution)/shard_map/while/body/eval_jaxpr/ppermute | solution.py:10
  368.9 9.1 %collective-permute-done = bf16[32,32,128]{2,0,1:T(8,128)(2,1)S(1)} collective-permute-done((bf16[32,32,128]{2,0,1:T(8,128)(2,1)S(1)}, bf16[32,32,128]{2,0,1:T(8,128)(2,1)S(1)}, u32[]{:S(2)}, u32[]{:S(2)}) %collective-permute-start) | collective-permute-done | bytes 262176 | tf_op jit(solution)/shard_map/while/body/eval_jaxpr/ppermute | solution.py:10
  385.1 9.1 %collective-permute-done = bf16[32,32,128]{2,0,1:T(8,128)(2,1)S(1)} collective-permute-done((bf16[32,32,128]{2,0,1:T(8,128)(2,1)S(1)}, bf16[32,32,128]{2,0,1:T(8,128)(2,1)S(1)}, u32[]{:S(2)}, u32[]{:S(2)}) %collective-permute-start) | collective-permute-done | bytes 262176 | tf_op jit(solution)/shard_map/while/body/eval_jaxpr/ppermute | solution.py:10
  417.5 9.1 %collective-permute-done = bf16[32,32,128]{2,0,1:T(8,128)(2,1)S(1)} collective-permute-done((bf16[32,32,128]{2,0,1:T(8,128)(2,1)S(1)}, bf16[32,32,128]{2,0,1:T(8,128)(2,1)S(1)}, u32[]{:S(2)}, u32[]{:S(2)}) %collective-permute-start) | collective-permute-done | bytes 262176 | tf_op jit(solution)/shard_map/while/body/eval_jaxpr/ppermute | solution.py:10
  433.7 10.0 %collective-permute-done = bf16[32,32,128]{2,0,1:T(8,128)(2,1)S(1)} collective-permute-done((bf16[32,32,128]{2,0,1:T(8,128)(2,1)S(1)}, bf16[32,32,128]{2,0,1:T(8,128)(2,1)S(1)}, u32[]{:S(2)}, u32[]{:S(2)}) %collective-permute-start) | collective-permute-done | bytes 262176 | tf_op jit(solution)/shard_map/while/body/eval_jaxpr/ppermute | solution.py:10
  450.8 11.1 %collective-permute-done = bf16[32,32,128]{2,0,1:T(8,128)(2,1)S(1)} collective-permute-done((bf16[32,32,128]{2,0,1:T(8,128)(2,1)S(1)}, bf16[32,32,128]{2,0,1:T(8,128)(2,1)S(1)}, u32[]{:S(2)}, u32[]{:S(2)}) %collective-permute-start) | collective-permute-done | bytes 262176 | tf_op jit(solution)/shard_map/while/body/eval_jaxpr/ppermute | solution.py:10
  469.0 12.6 %collective-permute-done = bf16[32,32,128]{2,0,1:T(8,128)(2,1)S(1)} collective-permute-done((bf16[32,32,128]{2,0,1:T(8,128)(2,1)S(1)}, bf16[32,32,128]{2,0,1:T(8,128)(2,1)S(1)}, u32[]{:S(2)}, u32[]{:S(2)}) %collective-permute-start) | collective-permute-done | bytes 262176 | tf_op jit(solution)/shard_map/while/body/eval_jaxpr/ppermute | solution.py:10
  488.7 9.4 %collective-permute-done = bf16[32,32,128]{2,0,1:T(8,128)(2,1)S(1)} collective-permute-done((bf16[32,32,128]{2,0,1:T(8,128)(2,1)S(1)}, bf16[32,32,128]{2,0,1:T(8,128)(2,1)S(1)}, u32[]{:S(2)}, u32[]{:S(2)}) %collective-permute-start) | collective-permute-done | bytes 262176 | tf_op jit(solution)/shard_map/while/body/eval_jaxpr/ppermute | solution.py:10
  505.2 9.6 %collective-permute-done = bf16[32,32,128]{2,0,1:T(8,128)(2,1)S(1)} collective-permute-done((bf16[32,32,128]{2,0,1:T(8,128)(2,1)S(1)}, bf16[32,32,128]{2,0,1:T(8,128)(2,1)S(1)}, u32[]{:S(2)}, u32[]{:S(2)}) %collective-permute-start) | collective-permute-done | bytes 262176 | tf_op jit(solution)/shard_map/while/body/eval_jaxpr/ppermute | solution.py:10
  521.5 20.6 %all-to-all-start.2 = ((f32[32,1,1024]{2,1,0:T(1,128)}), f32[32,1,1024]{2,1,0:T(1,128)S(1)}, u32[]{:S(2)}, u32[]{:S(2)}) async-start(f32[32,1,1024]{2,1,0:T(1,128)} %reshape.157), calls=%async_computation.2 | async-start | bytes 262144 | tf_op jit(solution)/shard_map/all_to_all | solution.py:107
  561.4 10.8 %all_to_all.54 = f32[4,1,8192]{2,1,0:T(1,128)S(1)} all-to-all(f32[4,1,8192]{2,1,0:T(1,128)S(1)} %reshape.159), channel_id=1, replica_groups=mesh['ctx'=32,'head'=4] {'head'}, dimensions={0} | all-to-all | bytes 262144 | tf_op jit(solution)/shard_map/all_to_all | solution.py:106
  581.5 158.5 %all-to-all-done.4 = bf16[32,32,32,128]{3,2,1,0:T(8,128)(2,1)} async-done(((bf16[32,32,32,128]{3,2,1,0:T(8,128)(2,1)}), bf16[32,32,32,128]{3,2,1,0:T(8,128)(2,1)}, u32[]{:S(2)}, u32[]{:S(2)}) %all-to-all-start.4) | async-done | bytes 8388640 | tf_op jit(solution)/shard_map/all_to_all | solution.py:99
  743.4 9.1 %copy.77 = bf16[32,32,32,128]{3,2,0,1:T(8,128)(2,1)} copy(bf16[32,32,32,128]{3,2,1,0:T(8,128)(2,1)} %all-to-all-done.4) | data formatting | bytes 16777216 | tf_op jit(solution)/shard_map/all_to_all | solution.py:99
  761.5 91.4 %all-to-all-done.5 = bf16[32,32,32,128]{3,2,0,1:T(8,128)(2,1)} async-done(((bf16[32,32,32,128]{3,2,0,1:T(8,128)(2,1)}), bf16[32,32,32,128]{3,2,0,1:T(8,128)(2,1)}, u32[]{:S(2)}, u32[]{:S(2)}) %all-to-all-start.5) | async-done | bytes 8388640 | tf_op jit(solution)/shard_map/all_to_all | solution.py:98
  852.8 11.4 %bitcast_convert_fusion = f32[32,4,8,32,128]{4,3,0,2,1:T(8,128)} fusion(bf16[32,32,32,128]{3,2,0,1:T(8,128)(2,1)} %all-to-all-done.5), kind=kLoop, calls=%fused_computation.57 | loop fusion | flops 4194304 | bytes 25165824 | tf_op jit(solution)/shard_map/convert_element_type | solution.py:60
  (467 shorter events, 374.9 us)
Async XLA Ops:
  116.3 10.7 %collective-permute-start = (bf16[32,32,128]{2,0,1:T(8,128)(2,1)S(1)}, bf16[32,32,128]{2,0,1:T(8,128)(2,1)S(1)}, u32[]{:S(2)}, u32[]{:S(2)}) collective-permute-start(bf16[32,32,128]{2,0,1:T(8,128)(2,1)S(1)} %get-tuple-element.456), channel_id=1, source_target_pairs={{124,0},{0,4},{4,8},{8,12},{12,16},{16,20},{20,24},{24,28},{28,32}... | collective-permute-start | bytes 786440 | tf_op jit(solution)/shard_map/while/body/eval_jaxpr/ppermute | solution.py:10
  132.6 10.7 %collective-permute-start = (bf16[32,32,128]{2,0,1:T(8,128)(2,1)S(1)}, bf16[32,32,128]{2,0,1:T(8,128)(2,1)S(1)}, u32[]{:S(2)}, u32[]{:S(2)}) collective-permute-start(bf16[32,32,128]{2,0,1:T(8,128)(2,1)S(1)} %get-tuple-element.456), channel_id=1, source_target_pairs={{124,0},{0,4},{4,8},{8,12},{12,16},{16,20},{20,24},{24,28},{28,32}... | collective-permute-start | bytes 786440 | tf_op jit(solution)/shard_map/while/body/eval_jaxpr/ppermute | solution.py:10
  165.0 10.7 %collective-permute-start = (bf16[32,32,128]{2,0,1:T(8,128)(2,1)S(1)}, bf16[32,32,128]{2,0,1:T(8,128)(2,1)S(1)}, u32[]{:S(2)}, u32[]{:S(2)}) collective-permute-start(bf16[32,32,128]{2,0,1:T(8,128)(2,1)S(1)} %get-tuple-element.456), channel_id=1, source_target_pairs={{124,0},{0,4},{4,8},{8,12},{12,16},{16,20},{20,24},{24,28},{28,32}... | collective-permute-start | bytes 786440 | tf_op jit(solution)/shard_map/while/body/eval_jaxpr/ppermute | solution.py:10
  181.2 10.7 %collective-permute-start = (bf16[32,32,128]{2,0,1:T(8,128)(2,1)S(1)}, bf16[32,32,128]{2,0,1:T(8,128)(2,1)S(1)}, u32[]{:S(2)}, u32[]{:S(2)}) collective-permute-start(bf16[32,32,128]{2,0,1:T(8,128)(2,1)S(1)} %get-tuple-element.456), channel_id=1, source_target_pairs={{124,0},{0,4},{4,8},{8,12},{12,16},{16,20},{20,24},{24,28},{28,32}... | collective-permute-start | bytes 786440 | tf_op jit(solution)/shard_map/while/body/eval_jaxpr/ppermute | solution.py:10
  197.4 11.4 %collective-permute-start = (bf16[32,32,128]{2,0,1:T(8,128)(2,1)S(1)}, bf16[32,32,128]{2,0,1:T(8,128)(2,1)S(1)}, u32[]{:S(2)}, u32[]{:S(2)}) collective-permute-start(bf16[32,32,128]{2,0,1:T(8,128)(2,1)S(1)} %get-tuple-element.456), channel_id=1, source_target_pairs={{124,0},{0,4},{4,8},{8,12},{12,16},{16,20},{20,24},{24,28},{28,32}... | collective-permute-start | bytes 786440 | tf_op jit(solution)/shard_map/while/body/eval_jaxpr/ppermute | solution.py:10
  214.3 12.9 %collective-permute-start = (bf16[32,32,128]{2,0,1:T(8,128)(2,1)S(1)}, bf16[32,32,128]{2,0,1:T(8,128)(2,1)S(1)}, u32[]{:S(2)}, u32[]{:S(2)}) collective-permute-start(bf16[32,32,128]{2,0,1:T(8,128)(2,1)S(1)} %get-tuple-element.456), channel_id=1, source_target_pairs={{124,0},{0,4},{4,8},{8,12},{12,16},{16,20},{20,24},{24,28},{28,32}... | collective-permute-start | bytes 786440 | tf_op jit(solution)/shard_map/while/body/eval_jaxpr/ppermute | solution.py:10
  232.8 14.1 %collective-permute-start = (bf16[32,32,128]{2,0,1:T(8,128)(2,1)S(1)}, bf16[32,32,128]{2,0,1:T(8,128)(2,1)S(1)}, u32[]{:S(2)}, u32[]{:S(2)}) collective-permute-start(bf16[32,32,128]{2,0,1:T(8,128)(2,1)S(1)} %get-tuple-element.456), channel_id=1, source_target_pairs={{124,0},{0,4},{4,8},{8,12},{12,16},{16,20},{20,24},{24,28},{28,32}... | collective-permute-start | bytes 786440 | tf_op jit(solution)/shard_map/while/body/eval_jaxpr/ppermute | solution.py:10
  252.4 12.7 %collective-permute-start = (bf16[32,32,128]{2,0,1:T(8,128)(2,1)S(1)}, bf16[32,32,128]{2,0,1:T(8,128)(2,1)S(1)}, u32[]{:S(2)}, u32[]{:S(2)}) collective-permute-start(bf16[32,32,128]{2,0,1:T(8,128)(2,1)S(1)} %get-tuple-element.456), channel_id=1, source_target_pairs={{124,0},{0,4},{4,8},{8,12},{12,16},{16,20},{20,24},{24,28},{28,32}... | collective-permute-start | bytes 786440 | tf_op jit(solution)/shard_map/while/body/eval_jaxpr/ppermute | solution.py:10
  270.7 11.8 %collective-permute-start = (bf16[32,32,128]{2,0,1:T(8,128)(2,1)S(1)}, bf16[32,32,128]{2,0,1:T(8,128)(2,1)S(1)}, u32[]{:S(2)}, u32[]{:S(2)}) collective-permute-start(bf16[32,32,128]{2,0,1:T(8,128)(2,1)S(1)} %get-tuple-element.456), channel_id=1, source_target_pairs={{124,0},{0,4},{4,8},{8,12},{12,16},{16,20},{20,24},{24,28},{28,32}... | collective-permute-start | bytes 786440 | tf_op jit(solution)/shard_map/while/body/eval_jaxpr/ppermute | solution.py:10
  334.9 10.6 %collective-permute-start = (bf16[32,32,128]{2,0,1:T(8,128)(2,1)S(1)}, bf16[32,32,128]{2,0,1:T(8,128)(2,1)S(1)}, u32[]{:S(2)}, u32[]{:S(2)}) collective-permute-start(bf16[32,32,128]{2,0,1:T(8,128)(2,1)S(1)} %get-tuple-element.456), channel_id=1, source_target_pairs={{124,0},{0,4},{4,8},{8,12},{12,16},{16,20},{20,24},{24,28},{28,32}... | collective-permute-start | bytes 786440 | tf_op jit(solution)/shard_map/while/body/eval_jaxpr/ppermute | solution.py:10
  351.1 10.7 %collective-permute-start = (bf16[32,32,128]{2,0,1:T(8,128)(2,1)S(1)}, bf16[32,32,128]{2,0,1:T(8,128)(2,1)S(1)}, u32[]{:S(2)}, u32[]{:S(2)}) collective-permute-start(bf16[32,32,128]{2,0,1:T(8,128)(2,1)S(1)} %get-tuple-element.456), channel_id=1, source_target_pairs={{124,0},{0,4},{4,8},{8,12},{12,16},{16,20},{20,24},{24,28},{28,32}... | collective-permute-start | bytes 786440 | tf_op jit(solution)/shard_map/while/body/eval_jaxpr/ppermute | solution.py:10
  367.3 10.7 %collective-permute-start = (bf16[32,32,128]{2,0,1:T(8,128)(2,1)S(1)}, bf16[32,32,128]{2,0,1:T(8,128)(2,1)S(1)}, u32[]{:S(2)}, u32[]{:S(2)}) collective-permute-start(bf16[32,32,128]{2,0,1:T(8,128)(2,1)S(1)} %get-tuple-element.456), channel_id=1, source_target_pairs={{124,0},{0,4},{4,8},{8,12},{12,16},{16,20},{20,24},{24,28},{28,32}... | collective-permute-start | bytes 786440 | tf_op jit(solution)/shard_map/while/body/eval_jaxpr/ppermute | solution.py:10
  383.5 10.7 %collective-permute-start = (bf16[32,32,128]{2,0,1:T(8,128)(2,1)S(1)}, bf16[32,32,128]{2,0,1:T(8,128)(2,1)S(1)}, u32[]{:S(2)}, u32[]{:S(2)}) collective-permute-start(bf16[32,32,128]{2,0,1:T(8,128)(2,1)S(1)} %get-tuple-element.456), channel_id=1, source_target_pairs={{124,0},{0,4},{4,8},{8,12},{12,16},{16,20},{20,24},{24,28},{28,32}... | collective-permute-start | bytes 786440 | tf_op jit(solution)/shard_map/while/body/eval_jaxpr/ppermute | solution.py:10
  415.9 10.7 %collective-permute-start = (bf16[32,32,128]{2,0,1:T(8,128)(2,1)S(1)}, bf16[32,32,128]{2,0,1:T(8,128)(2,1)S(1)}, u32[]{:S(2)}, u32[]{:S(2)}) collective-permute-start(bf16[32,32,128]{2,0,1:T(8,128)(2,1)S(1)} %get-tuple-element.456), channel_id=1, source_target_pairs={{124,0},{0,4},{4,8},{8,12},{12,16},{16,20},{20,24},{24,28},{28,32}... | collective-permute-start | bytes 786440 | tf_op jit(solution)/shard_map/while/body/eval_jaxpr/ppermute | solution.py:10
  432.1 11.5 %collective-permute-start = (bf16[32,32,128]{2,0,1:T(8,128)(2,1)S(1)}, bf16[32,32,128]{2,0,1:T(8,128)(2,1)S(1)}, u32[]{:S(2)}, u32[]{:S(2)}) collective-permute-start(bf16[32,32,128]{2,0,1:T(8,128)(2,1)S(1)} %get-tuple-element.456), channel_id=1, source_target_pairs={{124,0},{0,4},{4,8},{8,12},{12,16},{16,20},{20,24},{24,28},{28,32}... | collective-permute-start | bytes 786440 | tf_op jit(solution)/shard_map/while/body/eval_jaxpr/ppermute | solution.py:10
  449.2 12.7 %collective-permute-start = (bf16[32,32,128]{2,0,1:T(8,128)(2,1)S(1)}, bf16[32,32,128]{2,0,1:T(8,128)(2,1)S(1)}, u32[]{:S(2)}, u32[]{:S(2)}) collective-permute-start(bf16[32,32,128]{2,0,1:T(8,128)(2,1)S(1)} %get-tuple-element.456), channel_id=1, source_target_pairs={{124,0},{0,4},{4,8},{8,12},{12,16},{16,20},{20,24},{24,28},{28,32}... | collective-permute-start | bytes 786440 | tf_op jit(solution)/shard_map/while/body/eval_jaxpr/ppermute | solution.py:10
  467.4 14.1 %collective-permute-start = (bf16[32,32,128]{2,0,1:T(8,128)(2,1)S(1)}, bf16[32,32,128]{2,0,1:T(8,128)(2,1)S(1)}, u32[]{:S(2)}, u32[]{:S(2)}) collective-permute-start(bf16[32,32,128]{2,0,1:T(8,128)(2,1)S(1)} %get-tuple-element.456), channel_id=1, source_target_pairs={{124,0},{0,4},{4,8},{8,12},{12,16},{16,20},{20,24},{24,28},{28,32}... | collective-permute-start | bytes 786440 | tf_op jit(solution)/shard_map/while/body/eval_jaxpr/ppermute | solution.py:10
  487.1 11.0 %collective-permute-start = (bf16[32,32,128]{2,0,1:T(8,128)(2,1)S(1)}, bf16[32,32,128]{2,0,1:T(8,128)(2,1)S(1)}, u32[]{:S(2)}, u32[]{:S(2)}) collective-permute-start(bf16[32,32,128]{2,0,1:T(8,128)(2,1)S(1)} %get-tuple-element.456), channel_id=1, source_target_pairs={{124,0},{0,4},{4,8},{8,12},{12,16},{16,20},{20,24},{24,28},{28,32}... | collective-permute-start | bytes 786440 | tf_op jit(solution)/shard_map/while/body/eval_jaxpr/ppermute | solution.py:10
  503.7 11.1 %collective-permute-start = (bf16[32,32,128]{2,0,1:T(8,128)(2,1)S(1)}, bf16[32,32,128]{2,0,1:T(8,128)(2,1)S(1)}, u32[]{:S(2)}, u32[]{:S(2)}) collective-permute-start(bf16[32,32,128]{2,0,1:T(8,128)(2,1)S(1)} %get-tuple-element.456), channel_id=1, source_target_pairs={{124,0},{0,4},{4,8},{8,12},{12,16},{16,20},{20,24},{24,28},{28,32}... | collective-permute-start | bytes 786440 | tf_op jit(solution)/shard_map/while/body/eval_jaxpr/ppermute | solution.py:10
  521.5 27.3 %all-to-all-start.2 = ((f32[32,1,1024]{2,1,0:T(1,128)}), f32[32,1,1024]{2,1,0:T(1,128)S(1)}, u32[]{:S(2)}, u32[]{:S(2)}) async-start(f32[32,1,1024]{2,1,0:T(1,128)} %reshape.157), calls=%async_computation.2 | async-start | bytes 262144 | tf_op jit(solution)/shard_map/all_to_all | solution.py:107
  548.8 12.6 %all-to-all-start = ((f32[32,1,1024]{2,1,0:T(1,128)}), f32[32,1,1024]{2,1,0:T(1,128)S(1)}, u32[]{:S(2)}, u32[]{:S(2)}) async-start(f32[32,1,1024]{2,1,0:T(1,128)} %reshape.153), calls=%async_computation | async-start | bytes 262144 | tf_op jit(solution)/shard_map/all_to_all | solution.py:114
  572.2 167.8 %all-to-all-start.4 = ((bf16[32,32,32,128]{3,2,1,0:T(8,128)(2,1)}), bf16[32,32,32,128]{3,2,1,0:T(8,128)(2,1)}, u32[]{:S(2)}, u32[]{:S(2)}) async-start(bf16[32,32,32,128]{3,2,1,0:T(8,128)(2,1)} %get-tuple-element.275), calls=%async_computation.4 | async-start | bytes 16777216 | tf_op jit(solution)/shard_map/all_to_all | solution.py:99
  740.0 12.5 %all-to-all-start.1 = ((f32[4,1,8192]{2,1,0:T(1,128)}), f32[4,1,8192]{2,1,0:T(1,128)S(1)}, u32[]{:S(2)}, u32[]{:S(2)}) async-start(f32[4,1,8192]{2,1,0:T(1,128)} %reshape.155), calls=%async_computation.1 | async-start | bytes 262144 | tf_op jit(solution)/shard_map/all_to_all | solution.py:113
  752.5 100.3 %all-to-all-start.5 = ((bf16[32,32,32,128]{3,2,0,1:T(8,128)(2,1)}), bf16[32,32,32,128]{3,2,0,1:T(8,128)(2,1)}, u32[]{:S(2)}, u32[]{:S(2)}) async-start(bf16[32,32,32,128]{3,2,0,1:T(8,128)(2,1)} %copy.77), calls=%async_computation.5 | async-start | bytes 16777216 | tf_op jit(solution)/shard_map/all_to_all | solution.py:98
  (13 other events, 115.7 us)
where the time goes:
time: 874 us; the launch traced here: 873 us
  waiting for transfers between devices  512 us (59%)
  other arithmetic  100 us (11%)
  matrix products  97.9 us (11%)
  starting transfers between devices  76.2 us (9%)
  local copies, waits for them, and re-layouts  50.5 us (6%)
  loops' own time  23.1 us (3%)
  blocking collectives  10.8 us (1%)
    ppermute x31, waiting for transfers between devices, passed_along(): return lax.ppermute(block, axis, route)  252 us
    all_to_all x1, waiting for transfers between devices, per_device(): lax.all_to_all(buffers[0], 'ctx', split_axis=0, concat_axis=0, tiled=True)  159 us
    all_to_all x1, waiting for transfers between devices, per_device(): lax.all_to_all(lax.all_to_all(buffers[0], 'ctx', split_axis=0, concat_axi...  91.4 us
    dot_general x32, matrix products, block_partial(): jnp.einsum('rkgc,ckd->rkgd', probabilities.astype(jnp.bfloat16), value_ro...  59.9 us
    reduce_sum x32, other arithmetic, block_partial(): totals = jnp.sum(probabilities, axis=-1)  51.8 us
    dot_general x32, matrix products, block_partial(): jnp.einsum('rkgd,ckd->rkgc', grouped, key_rows, preferred_element_type=jn...  38 us
    ppermute x31, starting transfers between devices, passed_along(): return lax.ppermute(block, axis, route)  33.8 us
    another operation x1, loops' own time, per_device(): buffers = lax.fori_loop(1, shard_count, advance, (queries, buffers))[1]  23.1 us
  transfers between devices with their start and end apart: 36, of which 35 were waited for; matrix products, arithmetic and copies ran while one was open for 5% of the time, Pallas kernels for 0%

commit v1 on v0

v1 whole, which is shorter than its diff:
```python
import functools
import math

import jax
import jax.numpy as jnp
from jax import lax
from jax.experimental import pallas as pl
from jax.experimental.pallas import tpu as pltpu
from jax.sharding import Mesh, PartitionSpec as P

F32 = jnp.float32
BF16 = jnp.bfloat16
SCALE = math.log2(math.e) / math.sqrt(128)
HIDDEN = -1e30
SUM_LIMIT = 1e30
SLOTS = 1280
SPAN = 32
KEYS = SLOTS + SPAN
GROUP = 16
ROWS = SPAN * GROUP
BLOCKS = 8
SUB = 256
NOTE = 144
HALVES = 2


def times_transposed(a, b):
    return lax.dot_general(a, b, (((1,), (1,)), ((), ())), preferred_element_type=F32)


def times(a, b):
    return jnp.dot(a, b, preferred_element_type=F32)


def attend_kernel(
    lengths, key_start, query_start, place, *refs, head
):
    q_in = refs[:BLOCKS]
    own, left, right, far_k, far_v = refs[BLOCKS : BLOCKS + 5]
    out, q_ref, kv_ref, acc, top, fresh, sems = refs[BLOCKS + 5 :]
    copies = []
    for b in range(BLOCKS):
        copies.append((q_in[b].at[:, head * GROUP : (head + 1) * GROUP, :], q_ref.at[b]))
    for s, source in enumerate((own, left, right)):
        copies.append((source, kv_ref.at[s]))
    copies.append((far_k, kv_ref.at[3, 0]))
    copies.append((far_v, kv_ref.at[3, 1]))
    copies = [pltpu.make_async_copy(a, b, sems.at[n]) for n, (a, b) in enumerate(copies)]
    for copy in copies:
        copy.start()
    for copy in copies:
        copy.wait()

    lane = lax.broadcasted_iota(jnp.int32, (1, 128), 1)
    slot = lax.broadcasted_iota(jnp.int32, (128, 1), 0)
    begins = [jnp.int32(0)]
    for s in range(4):
        begins.append(begins[-1] + (lengths[s] + 127) // 128)
    count = begins[4]

    def half(index):
        shard, begin, length = jnp.int32(0), jnp.int32(0), lengths[0]
        for s in range(1, 4):
            later = index >= begins[s]
            shard = jnp.where(later, s, shard)
            begin = jnp.where(later, begins[s], begin)
            length = jnp.where(later, lengths[s], length)
        row = (index - begin) * 128
        exists = index < count
        filled = jnp.where(exists, length - row, 0)
        row = jnp.where(exists, row, 0)
        return shard, pl.multiple_of(row, 128), filled

    for s in range(4):
        for part in range(2):
            fresh[part, s * SPAN : (s + 1) * SPAN] = kv_ref[s, part, SLOTS:KEYS]
    position = jnp.zeros((1, 128), jnp.int32)
    for s in range(4):
        position = jnp.where(lane // SPAN == s, key_start[s] + lane - s * SPAN, position)

    def queries_of(r):
        first = (r % ROWS) // GROUP
        return q_ref[r // ROWS, first : first + SUB // GROUP].reshape(SUB, 128)

    def limit_of(block, first):
        token = lax.broadcasted_iota(jnp.int32, (SUB, 128), 0) // GROUP
        return token + (query_start[block] + first)

    ones = jnp.ones((128, 128), BF16)
    k_first = jnp.concatenate([fresh[0], kv_ref[0, 0, 0:128]], 0)
    v_first = jnp.concatenate([fresh[1], kv_ref[0, 1, 0:128]], 0)
    v_first = jnp.concatenate([v_first, jnp.concatenate([ones, ones], 0)], 1)
    for r in range(0, BLOCKS * ROWS, SUB):
        scores = times_transposed(queries_of(r), k_first)
        limit = limit_of(r // ROWS, (r % ROWS) // GROUP)
        s0 = jnp.where(position <= limit, scores[:, :128], HIDDEN)
        s1 = jnp.where(lane < lengths[0], scores[:, 128:], HIDDEN)
        largest = jnp.max(jnp.maximum(s0, s1), axis=1, keepdims=True)
        base = jnp.broadcast_to(largest * SCALE, (SUB, 128))
        top[r : r + SUB] = base
        p0 = jnp.exp2(s0 * SCALE - base).astype(BF16)
        p1 = jnp.exp2(s1 * SCALE - base).astype(BF16)
        acc[r : r + SUB] = times(jnp.concatenate([p0, p1], 1), v_first)

    def step(number, carry):
        parts = [half(HALVES * number + g + 1) for g in range(HALVES)]
        k = jnp.concatenate([kv_ref[s, 0, pl.ds(row, 128)] for s, row, _ in parts], 0)
        v = jnp.concatenate(
            [
                jnp.concatenate(
                    [
                        jnp.where(slot < filled, kv_ref[s, 1, pl.ds(row, 128)], 0),
                        jnp.where(slot < filled, ones, 0),
                    ],
                    1,
                )
                for s, row, filled in parts
            ],
            0,
        )
        for r in range(0, BLOCKS * ROWS, SUB):
            scores = times_transposed(queries_of(r), k)
            base = top[r : r + SUB]
            probs = [
                jnp.exp2(scores[:, g * 128 : (g + 1) * 128] * SCALE - base).astype(BF16)
                for g in range(HALVES)
            ]
            acc[r : r + SUB] += times(jnp.concatenate(probs, 1), v)
        return carry

    lax.fori_loop(0, (count - 1 + HALVES - 1) // HALVES, step, 0)

    wrong = jnp.zeros((8, 128), F32)
    for r in range(0, BLOCKS * ROWS, 8):
        wrong = jnp.maximum(wrong, jnp.where(acc[r : r + 8, 128:] < SUM_LIMIT, 0.0, 1.0))

    @pl.when(jnp.max(wrong) > 0.5)
    def _():
        def redo(tile, carry):
            block, first = tile // 2, (tile % 2) * (SUB // GROUP)
            rows = pl.ds(pl.multiple_of(tile * SUB, SUB), SUB)
            q = q_ref[block, pl.ds(first, SUB // GROUP)].reshape(SUB, 128)

            def absorb(scores, v, state):
                old, total = state
                new = jnp.maximum(old, jnp.max(scores, axis=1, keepdims=True) * SCALE)
                shrink = jnp.exp2(old - new)
                p = jnp.exp2(scores * SCALE - new)
                total = total * shrink + jnp.sum(p, axis=1, keepdims=True)
                acc[rows, 0:128] = acc[rows, 0:128] * shrink + times(p.astype(BF16), v)
                return new, total

            acc[rows] = jnp.zeros((SUB, 256), F32)
            state = (jnp.full((SUB, 1), HIDDEN, F32), jnp.zeros((SUB, 1), F32))

            def more(index, state):
                s, row, filled = half(index)
                scores = times_transposed(q, kv_ref[s, 0, pl.ds(row, 128)])
                scores = jnp.where(lane < filled, scores, HIDDEN)
                return absorb(scores, kv_ref[s, 1, pl.ds(row, 128)], state)

            state = lax.fori_loop(0, count, more, state)
            scores = times_transposed(q, fresh[0])
            scores = jnp.where(position <= limit_of(block, first), scores, HIDDEN)
            base, total = absorb(scores, fresh[1], state)
            top[rows] = jnp.broadcast_to(base, (SUB, 128))
            acc[rows, 128:256] = jnp.broadcast_to(total, (SUB, 128))
            return carry

        lax.fori_loop(0, BLOCKS * ROWS // SUB, redo, 0)

    diagonal = lax.broadcasted_iota(jnp.int32, (128, 128), 0) == lane
    for b in range(BLOCKS):
        for quarter in range(4):
            r = b * ROWS + quarter * 128
            total = acc[r : r + 128, 128:]
            out[place[b], quarter, 0:128] = (acc[r : r + 128, 0:128] / total).astype(BF16)
            lse = top[r : r + 128] + jnp.log2(total)
            lse = jnp.sum(jnp.where(diagonal, lse, 0.0), axis=0, keepdims=True)
            high = lse.astype(BF16).astype(F32)
            middle = (lse - high).astype(BF16).astype(F32)
            low = lse - high - middle
            row = lax.broadcasted_iota(jnp.int32, (16, 128), 0)
            note = jnp.where(row == 0, high, jnp.where(row == 1, middle, jnp.where(row == 2, low, 0.0)))
            out[place[b], quarter, 128:NOTE] = note.astype(BF16)


def attend(scalars, queries, kv, head):
    return pl.pallas_call(
        functools.partial(attend_kernel, head=head),
        out_shape=jax.ShapeDtypeStruct((BLOCKS, 4, NOTE, 128), BF16),
        in_specs=[pl.BlockSpec(memory_space=pltpu.SMEM)] * 4
        + [pl.BlockSpec(memory_space=pl.ANY)] * (BLOCKS + 5),
        out_specs=pl.BlockSpec(memory_space=pltpu.VMEM),
        scratch_shapes=[
            pltpu.VMEM((BLOCKS, SPAN, GROUP, 128), BF16),
            pltpu.VMEM((4, 2, KEYS, 128), BF16),
            pltpu.VMEM((BLOCKS * ROWS, 256), F32),
            pltpu.VMEM((BLOCKS * ROWS, 128), F32),
            pltpu.VMEM((2, 128, 128), BF16),
            pltpu.SemaphoreType.DMA((BLOCKS + 5,)),
        ],
        compiler_params=pltpu.CompilerParams(vmem_limit_bytes=40 << 20),
        cost_estimate=pl.CostEstimate(
            flops=2 * 2 * BLOCKS * ROWS * 4 * KEYS * 256,
            bytes_accessed=8 << 20,
            transcendentals=0,
        ),
        name="attend",
    )(*scalars, *queries, *kv)


def merge_kernel(first, second, out):
    eye = lax.broadcasted_iota(jnp.int32, (128, 128), 0) == lax.broadcasted_iota(jnp.int32, (128, 128), 1)
    for source in range(4):
        for head, ref in enumerate((first, second)):
            lse = []
            for b in range(BLOCKS):
                note = ref[b * 4 + source, 128:NOTE].astype(F32)
                lse.append(note[0:1] + note[1:2] + note[2:3])
            largest = functools.reduce(jnp.maximum, lse)
            weights = [jnp.exp2(x - largest) for x in lse]
            total = functools.reduce(jnp.add, weights)
            left, right = [], []
            for b in range(BLOCKS):
                weight = jnp.broadcast_to(weights[b] / total, (128, 128))
                high = weight.astype(BF16)
                low = (weight - high.astype(F32)).astype(BF16)
                left += [jnp.where(eye, high, 0), jnp.where(eye, low, 0)]
                partial = ref[b * 4 + source, 0:128]
                right += [partial, partial]
            merged = times(jnp.concatenate(left, 1), jnp.concatenate(right, 0))
            begin = source * 32 + head * GROUP
            out[:, begin : begin + GROUP] = merged.astype(BF16).reshape(8, GROUP, 128)


def merge(first, second):
    return pl.pallas_call(
        merge_kernel,
        out_shape=jax.ShapeDtypeStruct((8, 128, 128), BF16),
        in_specs=[pl.BlockSpec(memory_space=pltpu.VMEM)] * 2,
        out_specs=pl.BlockSpec(memory_space=pltpu.VMEM),
        compiler_params=pltpu.CompilerParams(vmem_limit_bytes=32 << 20),
        name="merge",
    )(first, second)


def moved(block, axis, distance):
    size = lax.axis_size(axis)
    return lax.ppermute(block, axis, [(i, (i + distance) % size) for i in range(size)])


def per_device(queries, cache_keys, cache_values, new_keys, new_values, lengths, span_offset):
    x, z, y = lax.axis_index("x"), lax.axis_index("z"), lax.axis_index("y")

    def packed(head):
        k = jnp.concatenate([cache_keys[:, head], new_keys[:, head]], 0)
        v = jnp.concatenate([cache_values[:, head], new_values[:, head]], 0)
        return jnp.stack([k, v])

    def gathered(own):
        left, right = moved(own, "y", 1), moved(own, "y", -1)
        return own, left, right, moved(left[0], "y", 1), moved(right[1], "y", -1)

    all_lengths = lax.all_gather(lengths[0], "y")
    beside = moved(queries, "z", 1)
    blocks, homes = [], []
    for dz, block in enumerate((queries, beside)):
        for dx in (0, 1, -1, 2):
            blocks.append(moved(block, "x", -dx) if dx else block)
            homes.append(((x + dx) % 4, (z + dz) % 2))
    place = jnp.stack([hx * 2 + hz for hx, hz in homes]).astype(jnp.int32)
    query_start = jnp.stack([(hx * 8 + hz * 4 + y) * SPAN for hx, hz in homes]).astype(jnp.int32) + span_offset
    shards = jnp.stack([y, (y - 1) % 4, (y + 1) % 4, (y + 2) % 4]).astype(jnp.int32)
    key_start = (x * 8 + z * 4 + shards) * SPAN
    scalars = (all_lengths[shards], key_start, query_start, place)

    kv = [gathered(packed(head)) for head in range(2)]
    partials = []
    for head in range(2):
        partial = attend(scalars, blocks, kv[head], head)
        partials.append(
            lax.all_to_all(
                partial.reshape(BLOCKS * 4, NOTE, 128), ("x", "z", "head"), 0, 0, tiled=True
            )
        )
    return merge(*partials)


def solution(mesh):
    inner = Mesh(mesh.devices.reshape(4, 2, 4, 4), ("x", "z", "y", "head"))
    context = ("x", "z", "y")
    return jax.shard_map(
        per_device,
        mesh=inner,
        in_specs=(
            P(context, "head", None),
            P(context, "head", None),
            P(context, "head", None),
            P(context, "head", None),
            P(context, "head", None),
            P(context),
            P(),
        ),
        out_specs=P((*context, "head"), None, None),
        check_vma=False,
    )
```

time: 874 us -> 441 us (0.50)
  the two profiles are of different devices: /device:TPU:24 before, /device:TPU:9 now
where the time goes in v1:
time: 441 us; the launch traced here: 432 us
  Pallas kernels  321 us (73%)
  blocking collectives  37.7 us (9%)
  starting transfers between devices  34.2 us (8%)
  local copies, waits for them, and re-layouts  24.4 us (6%)
  waiting for transfers between devices  10.8 us (2%)
    pallas_call x2, Pallas kernels, attend(): pl.pallas_call(functools.partial(attend_kernel, head=head), out_shape=jax...  319 us
    all_to_all x1, blocking collectives, per_device(): lax.all_to_all(partial.reshape(BLOCKS * 4, NOTE, 128), ('x', 'z', 'head')...  23.5 us
    ppermute x15, starting transfers between devices, moved(): lax.ppermute(block, axis, [(i, (i + distance) % size) for i in range(size)])  20.6 us
    unnamed x53, local copies, waits for them, and re-layouts  15.3 us
    unnamed x1, blocking collectives  14.2 us
    all_to_all x1, starting transfers between devices, per_device(): lax.all_to_all(partial.reshape(BLOCKS * 4, NOTE, 128), ('x', 'z', 'head')...  13.6 us
    ppermute x15, waiting for transfers between devices, moved(): lax.ppermute(block, axis, [(i, (i + distance) % size) for i in range(size)])  10.8 us
  transfers between devices with their start and end apart: 16, of which 2 were waited for; matrix products, arithmetic and copies ran while one was open for 3% of the time, Pallas kernels for 74%

profile of v1, /device:TPU:9, one launch (start us, length us, event | category | flops | bytes accessed | tf_op | source)
XLA Modules:
  0.0 432.4 jit_solution(11401663968515117941)
XLA Ops:
  0.0 1.6 collective-permute-start.3
  1.6 2.7 collective-permute-start.2
  6.4 2.4 fusion.2
  11.8 1.3 collective-permute-start.7
  15.7 14.2 %all-reduce = s32[4]{0:T(128)S(1)} all-reduce(s32[4]{0:T(128)S(1)} %dynamic-update-slice), channel_id=1, replica_groups=mesh['x'=4,'z'=2,'y'=4,'head'=4] {'y'}, use_global_device_ids=true, to_apply=%add | all-reduce | flops 4 | bytes 32
  30.7 1.7 maximum_bitcast_fusion.2
  32.7 1.1 pad_maximum_fusion.1.refs_8_
  33.8 1.1 collective-permute-start.12
  35.5 2.4 collective-permute-start
  38.0 8.9 %collective-permute-done.12.refs_10_ = bf16[2,1312,128]{2,1,0:T(8,128)(2,1)S(1)} collective-permute-done((bf16[2,1312,128]{2,1,0:T(8,128)(2,1)S(1)}, bf16[2,1312,128]{2,1,0:T(8,128)(2,1)S(1)}, u32[]{:S(2)}, u32[]{:S(2)}) %collective-permute-start.12) | collective-permute-done | bytes 671776 | tf_op jit(solution)/shard_map/ppermute | solution.py:250
  46.8 1.7 collective-permute-start.6
  49.3 1.2 collective-permute-start.5
  50.5 1.5 collective-permute-start.4
  52.0 1.4 collective-permute-start.10
  55.3 2.9 collective-permute-start.14
  58.2 1.3 collective-permute-start.13
  59.6 1.9 collective-permute-done.9.refs_11_
  63.4 159.9 %attend.2 = bf16[8,4,144,128]{3,2,1,0:T(8,128)(2,1)} custom-call(s32[4]{0:T(128)S(1)} %gather_fusion, s32[4]{0:T(128)S(1)} %fusion.1.key_start, s32[8]{0:T(128)S(1)} %broadcast_add_fusion.query_start, s32[8]{0:T(128)S(1)} %stack.124.place, bf16[32,32,128]{2,1,0:T(8,128)(2,1)S(1)} %copy-done.6, bf16[32,32,128]{2,1,0:T(8,128)(2,1)S(1)} %collective-permute-done.refs_1_, ...), custom_call_target="tpu_custom_call" | custom-call | flops 22011707392 | bytes 8388608 | tf_op jit(solution)/shard_map/attend/pallas_call | solution.py:189
  224.0 13.6 %all-to-all-start = ((bf16[32,144,128]{2,1,0:T(8,128)(2,1)}), bf16[32,144,128]{2,1,0:T(8,128)(2,1)S(1)}, u32[]{:S(2)}, u32[]{:S(2)}) async-start(bf16[32,144,128]{2,1,0:T(8,128)(2,1)} %bitcast.34), calls=%async_computation | async-start | bytes 2359296 | tf_op jit(solution)/shard_map/all_to_all | solution.py:283
  238.4 1.1 copy-done.1
  239.5 1.1 copy-done.3
  248.2 158.7 %attend.3 = bf16[8,4,144,128]{3,2,1,0:T(8,128)(2,1)S(1)} custom-call(s32[4]{0:T(128)S(1)} %gather_fusion, s32[4]{0:T(128)S(1)} %fusion.1.key_start, s32[8]{0:T(128)S(1)} %broadcast_add_fusion.query_start, s32[8]{0:T(128)S(1)} %stack.124.place, bf16[32,32,128]{2,1,0:T(8,128)(2,1)S(1)} %copy-done.7, bf16[32,32,128]{2,1,0:T(8,128)(2,1)S(1)} %copy-done.15, ...), custom_call_target="tpu_custom_call" | custom-call | flops 22011707392 | bytes 8388608 | tf_op jit(solution)/shard_map/attend/pallas_call | solution.py:189
  406.9 23.5 %all_to_all.10.second = bf16[32,144,128]{2,1,0:T(8,128)(2,1)S(1)} all-to-all(bf16[32,144,128]{2,1,0:T(8,128)(2,1)S(1)} %bitcast.61), channel_id=1, replica_groups=mesh['x'=4,'z'=2,'y'=4,'head'=4] {'x','z','head'}, dimensions={0} | all-to-all | bytes 2359296 | tf_op jit(solution)/shard_map/all_to_all | solution.py:283
  430.4 2.0 merge.1
  (91 shorter events, 21.5 us)
Async XLA Ops:
  0.0 35.5 %collective-permute-start.3 = (bf16[32,32,128]{2,1,0:T(8,128)(2,1)}, bf16[32,32,128]{2,1,0:T(8,128)(2,1)}, u32[]{:S(2)}, u32[]{:S(2)}) collective-permute-start(bf16[32,32,128]{2,1,0:T(8,128)(2,1)} %refs_0_.3), channel_id=1, source_target_pairs={{0,16},{16,0},{1,17},{17,1},{2,18},{18,2},{3,19},{19,3},{4,20},{20... | collective-permute-start | bytes 786440 | tf_op jit(solution)/shard_map/ppermute | solution.py:250
  1.6 47.7 %collective-permute-start.2 = (bf16[32,32,128]{2,1,0:T(8,128)(2,1)}, bf16[32,32,128]{2,1,0:T(8,128)(2,1)S(1)}, u32[]{:S(2)}, u32[]{:S(2)}) collective-permute-start(bf16[32,32,128]{2,1,0:T(8,128)(2,1)} %refs_0_.3), channel_id=1, source_target_pairs={{0,64},{32,96},{64,0},{96,32},{1,65},{33,97},{65,1},{97,33},{2,66}... | collective-permute-start | bytes 786440 | tf_op jit(solution)/shard_map/ppermute | solution.py:250
  4.4 46.2 %collective-permute-start.1 = (bf16[32,32,128]{2,1,0:T(8,128)(2,1)}, bf16[32,32,128]{2,1,0:T(8,128)(2,1)S(1)}, u32[]{:S(2)}, u32[]{:S(2)}) collective-permute-start(bf16[32,32,128]{2,1,0:T(8,128)(2,1)} %refs_0_.3), channel_id=1, source_target_pairs={{0,32},{32,64},{64,96},{96,0},{1,33},{33,65},{65,97},{97,1},{2,34}... | collective-permute-start | bytes 786440 | tf_op jit(solution)/shard_map/ppermute | solution.py:250
  11.5 21.1 %copy-start.23 = (bf16[1280,128]{1,0:T(8,128)(2,1)S(1)}, bf16[1280,128]{1,0:T(8,128)(2,1)}, u32[]{:S(2)}) copy-start(bf16[1280,128]{1,0:T(8,128)(2,1)} %get-tuple-element.15) | copy-start | bytes 983044
  11.6 22.3 %collective-permute-start.8 = (bf16[2,1312,128]{2,1,0:T(8,128)(2,1)S(1)}, bf16[2,1312,128]{2,1,0:T(8,128)(2,1)S(1)}, u32[]{:S(2)}, u32[]{:S(2)}) collective-permute-start(bf16[2,1312,128]{2,1,0:T(8,128)(2,1)S(1)} %pad_maximum_fusion.refs_8_), channel_id=1, source_target_pairs={{0,12},{4,0},{8,4},{12,8},{1,13},{5,1},{9,5},{13,9},{2,14},{6,2},{... | collective-permute-start | bytes 2015240 | tf_op jit(solution)/shard_map/ppermute | solution.py:250
  11.8 23.1 %collective-permute-start.7 = (bf16[2,1312,128]{2,1,0:T(8,128)(2,1)S(1)}, bf16[2,1312,128]{2,1,0:T(8,128)(2,1)S(1)}, u32[]{:S(2)}, u32[]{:S(2)}) collective-permute-start(bf16[2,1312,128]{2,1,0:T(8,128)(2,1)S(1)} %pad_maximum_fusion.refs_8_), channel_id=1, source_target_pairs={{0,4},{4,8},{8,12},{12,0},{1,5},{5,9},{9,13},{13,1},{2,6},{6,10},{... | collective-permute-start | bytes 2015240 | tf_op jit(solution)/shard_map/ppermute | solution.py:250
  32.7 2.8 copy-start.6
  33.8 13.0 %collective-permute-start.12 = (bf16[2,1312,128]{2,1,0:T(8,128)(2,1)S(1)}, bf16[2,1312,128]{2,1,0:T(8,128)(2,1)S(1)}, u32[]{:S(2)}, u32[]{:S(2)}) collective-permute-start(bf16[2,1312,128]{2,1,0:T(8,128)(2,1)S(1)} %pad_maximum_fusion.1.refs_8_), channel_id=1, source_target_pairs={{0,12},{4,0},{8,4},{12,8},{1,13},{5,1},{9,5},{13,9},{2,14},{6,2},{... | collective-permute-start | bytes 2015240 | tf_op jit(solution)/shard_map/ppermute | solution.py:250
  34.9 18.5 %collective-permute-start.11 = (bf16[2,1312,128]{2,1,0:T(8,128)(2,1)S(1)}, bf16[2,1312,128]{2,1,0:T(8,128)(2,1)S(1)}, u32[]{:S(2)}, u32[]{:S(2)}) collective-permute-start(bf16[2,1312,128]{2,1,0:T(8,128)(2,1)S(1)} %pad_maximum_fusion.1.refs_8_), channel_id=1, source_target_pairs={{0,4},{4,8},{8,12},{12,0},{1,5},{5,9},{9,13},{13,1},{2,6},{6,10},{... | collective-permute-start | bytes 2015240 | tf_op jit(solution)/shard_map/ppermute | solution.py:250
  35.5 16.5 %collective-permute-start = (bf16[32,32,128]{2,1,0:T(8,128)(2,1)S(1)}, bf16[32,32,128]{2,1,0:T(8,128)(2,1)S(1)}, u32[]{:S(2)}, u32[]{:S(2)}) collective-permute-start(bf16[32,32,128]{2,1,0:T(8,128)(2,1)S(1)} %copy-done.6), channel_id=1, source_target_pairs={{0,96},{32,0},{64,32},{96,64},{1,97},{33,1},{65,33},{97,65},{2,98}... | collective-permute-start | bytes 786440 | tf_op jit(solution)/shard_map/ppermute | solution.py:250
  46.8 6.6 %copy-start = (bf16[2,1312,128]{2,1,0:T(8,128)(2,1)}, bf16[2,1312,128]{2,1,0:T(8,128)(2,1)S(1)}, u32[]{:S(2)}) copy-start(bf16[2,1312,128]{2,1,0:T(8,128)(2,1)S(1)} %collective-permute-done.12.refs_10_) | copy-start | bytes 2015236
  46.8 8.5 %collective-permute-start.6 = (bf16[32,32,128]{2,1,0:T(8,128)(2,1)}, bf16[32,32,128]{2,1,0:T(8,128)(2,1)S(1)}, u32[]{:S(2)}, u32[]{:S(2)}) collective-permute-start(bf16[32,32,128]{2,1,0:T(8,128)(2,1)} %collective-permute-done.3.refs_4_), channel_id=1, source_target_pairs={{0,64},{32,96},{64,0},{96,32},{1,65},{33,97},{65,1},{97,33},{2,66}... | collective-permute-start | bytes 786440 | tf_op jit(solution)/shard_map/ppermute | solution.py:250
  49.3 8.9 %copy-start.8 = (bf16[32,32,128]{2,1,0:T(8,128)(2,1)}, bf16[32,32,128]{2,1,0:T(8,128)(2,1)S(1)}, u32[]{:S(2)}) copy-start(bf16[32,32,128]{2,1,0:T(8,128)(2,1)S(1)} %collective-permute-done.2.refs_3_) | copy-start | bytes 786436
  49.3 8.9 %collective-permute-start.5 = (bf16[32,32,128]{2,1,0:T(8,128)(2,1)}, bf16[32,32,128]{2,1,0:T(8,128)(2,1)S(1)}, u32[]{:S(2)}, u32[]{:S(2)}) collective-permute-start(bf16[32,32,128]{2,1,0:T(8,128)(2,1)} %collective-permute-done.3.refs_4_), channel_id=1, source_target_pairs={{0,32},{32,64},{64,96},{96,0},{1,33},{33,65},{65,97},{97,1},{2,34}... | collective-permute-start | bytes 786440 | tf_op jit(solution)/shard_map/ppermute | solution.py:250
  50.5 3.9 copy-start.11
  50.5 9.0 %collective-permute-start.4 = (bf16[32,32,128]{2,1,0:T(8,128)(2,1)}, bf16[32,32,128]{2,1,0:T(8,128)(2,1)S(1)}, u32[]{:S(2)}, u32[]{:S(2)}) collective-permute-start(bf16[32,32,128]{2,1,0:T(8,128)(2,1)} %collective-permute-done.3.refs_4_), channel_id=1, source_target_pairs={{0,96},{32,0},{64,32},{96,64},{1,97},{33,1},{65,33},{97,65},{2,98}... | collective-permute-start | bytes 786440 | tf_op jit(solution)/shard_map/ppermute | solution.py:250
  52.0 7.6 %collective-permute-start.10 = (bf16[1312,128]{1,0:T(8,128)(2,1)S(1)}, bf16[1312,128]{1,0:T(8,128)(2,1)S(1)}, u32[]{:S(2)}, u32[]{:S(2)}) collective-permute-start(bf16[1312,128]{1,0:T(8,128)(2,1)S(1)} %slice_bitcast_fusion.2), channel_id=1, source_target_pairs={{0,12},{4,0},{8,4},{12,8},{1,13},{5,1},{9,5},{13,9},{2,14},{6,2},{... | collective-permute-start | bytes 1007624 | tf_op jit(solution)/shard_map/ppermute | solution.py:250
  53.4 8.0 %collective-permute-start.9 = (bf16[1312,128]{1,0:T(8,128)(2,1)S(1)}, bf16[1312,128]{1,0:T(8,128)(2,1)S(1)}, u32[]{:S(2)}, u32[]{:S(2)}) collective-permute-start(bf16[1312,128]{1,0:T(8,128)(2,1)S(1)} %slice_bitcast_fusion.3), channel_id=1, source_target_pairs={{0,4},{4,8},{8,12},{12,0},{1,5},{5,9},{9,13},{13,1},{2,6},{6,10},{... | collective-permute-start | bytes 1007624 | tf_op jit(solution)/shard_map/ppermute | solution.py:250
  55.3 168.0 %copy-start.16 = (bf16[32,32,128]{2,1,0:T(8,128)(2,1)}, bf16[32,32,128]{2,1,0:T(8,128)(2,1)S(1)}, u32[]{:S(2)}) copy-start(bf16[32,32,128]{2,1,0:T(8,128)(2,1)S(1)} %collective-permute-done.6.refs_7_) | copy-start | bytes 786436
  55.3 182.3 %collective-permute-start.14 = (bf16[1312,128]{1,0:T(8,128)(2,1)}, bf16[1312,128]{1,0:T(8,128)(2,1)S(1)}, u32[]{:S(2)}, u32[]{:S(2)}) collective-permute-start(bf16[1312,128]{1,0:T(8,128)(2,1)} %slice_bitcast_fusion), channel_id=1, source_target_pairs={{0,12},{4,0},{8,4},{12,8},{1,13},{5,1},{9,5},{13,9},{2,14},{6,2},{... | collective-permute-start | bytes 1007624 | tf_op jit(solution)/shard_map/ppermute | solution.py:250
  58.2 165.1 %copy-start.18 = (bf16[32,32,128]{2,1,0:T(8,128)(2,1)}, bf16[32,32,128]{2,1,0:T(8,128)(2,1)S(1)}, u32[]{:S(2)}) copy-start(bf16[32,32,128]{2,1,0:T(8,128)(2,1)S(1)} %collective-permute-done.5.refs_6_) | copy-start | bytes 786436
  58.2 179.4 %collective-permute-start.13 = (bf16[1312,128]{1,0:T(8,128)(2,1)}, bf16[1312,128]{1,0:T(8,128)(2,1)S(1)}, u32[]{:S(2)}, u32[]{:S(2)}) collective-permute-start(bf16[1312,128]{1,0:T(8,128)(2,1)} %slice_bitcast_fusion.1), channel_id=1, source_target_pairs={{0,4},{4,8},{8,12},{12,0},{1,5},{5,9},{9,13},{13,1},{2,6},{6,10},{... | collective-permute-start | bytes 1007624 | tf_op jit(solution)/shard_map/ppermute | solution.py:250
  59.6 163.7 %copy-start.20 = (bf16[32,32,128]{2,1,0:T(8,128)(2,1)}, bf16[32,32,128]{2,1,0:T(8,128)(2,1)S(1)}, u32[]{:S(2)}) copy-start(bf16[32,32,128]{2,1,0:T(8,128)(2,1)S(1)} %collective-permute-done.4.refs_5_) | copy-start | bytes 786436
  224.0 182.9 %all-to-all-start = ((bf16[32,144,128]{2,1,0:T(8,128)(2,1)}), bf16[32,144,128]{2,1,0:T(8,128)(2,1)S(1)}, u32[]{:S(2)}, u32[]{:S(2)}) async-start(bf16[32,144,128]{2,1,0:T(8,128)(2,1)} %bitcast.34), calls=%async_computation | async-start | bytes 2359296 | tf_op jit(solution)/shard_map/all_to_all | solution.py:283
  (17 other events, 18.7 us)

commit v2 on v1

--- a/solution.py
+++ b/solution.py
@@ -16,12 +16,13 @@
 SLOTS = 1280
 SPAN = 32
 KEYS = SLOTS + SPAN
+PACKED = KEYS + 16
 GROUP = 16
 ROWS = SPAN * GROUP
 BLOCKS = 8
 SUB = 256
 NOTE = 144
-HALVES = 2
+HALVES = 8
 
 
 def times_transposed(a, b):
@@ -33,18 +34,16 @@
 
 
 def attend_kernel(
-    lengths, key_start, query_start, place, *refs, head
+    key_start, query_start, place, *refs, head
 ):
-    q_in = refs[:BLOCKS]
-    own, left, right, far_k, far_v = refs[BLOCKS : BLOCKS + 5]
-    out, q_ref, kv_ref, acc, top, fresh, sems = refs[BLOCKS + 5 :]
+    q_in = refs[:4]
+    shards = refs[4:8]
+    out, q_ref, kv_ref, acc, top, fresh, sums, sems = refs[8:]
     copies = []
     for b in range(BLOCKS):
-        copies.append((q_in[b].at[:, head * GROUP : (head + 1) * GROUP, :], q_ref.at[b]))
-    for s, source in enumerate((own, left, right)):
+        copies.append((q_in[b // 2].at[b % 2, :, head * GROUP : (head + 1) * GROUP, :], q_ref.at[b]))
+    for s, source in enumerate(shards):
         copies.append((source, kv_ref.at[s]))
-    copies.append((far_k, kv_ref.at[3, 0]))
-    copies.append((far_v, kv_ref.at[3, 1]))
     copies = [pltpu.make_async_copy(a, b, sems.at[n]) for n, (a, b) in enumerate(copies)]
     for copy in copies:
         copy.start()
@@ -53,6 +52,10 @@
 
     lane = lax.broadcasted_iota(jnp.int32, (1, 128), 1)
     slot = lax.broadcasted_iota(jnp.int32, (128, 1), 0)
+    lengths = []
+    for s in range(4):
+        digits = kv_ref[s, 0, KEYS:PACKED].astype(F32)
+        lengths.append((jnp.max(digits[0:1]) * 16.0 + jnp.max(digits[1:2])).astype(jnp.int32))
     begins = [jnp.int32(0)]
     for s in range(4):
         begins.append(begins[-1] + (lengths[s] + 127) // 128)
@@ -102,8 +105,8 @@
         p1 = jnp.exp2(s1 * SCALE - base).astype(BF16)
         acc[r : r + SUB] = times(jnp.concatenate([p0, p1], 1), v_first)
 
-    def step(number, carry):
-        parts = [half(HALVES * number + g + 1) for g in range(HALVES)]
+    def step(first, halves):
+        parts = [half(first + g) for g in range(halves)]
         k = jnp.concatenate([kv_ref[s, 0, pl.ds(row, 128)] for s, row, _ in parts], 0)
         v = jnp.concatenate(
             [
@@ -123,16 +126,38 @@
             base = top[r : r + SUB]
             probs = [
                 jnp.exp2(scores[:, g * 128 : (g + 1) * 128] * SCALE - base).astype(BF16)
-                for g in range(HALVES)
+                for g in range(halves)
             ]
             acc[r : r + SUB] += times(jnp.concatenate(probs, 1), v)
+
+    def full_step(number, carry):
+        step(HALVES * number + 1, HALVES)
         return carry
 
-    lax.fori_loop(0, (count - 1 + HALVES - 1) // HALVES, step, 0)
-
-    wrong = jnp.zeros((8, 128), F32)
-    for r in range(0, BLOCKS * ROWS, 8):
-        wrong = jnp.maximum(wrong, jnp.where(acc[r : r + 8, 128:] < SUM_LIMIT, 0.0, 1.0))
+    steps = count // HALVES
+    lax.fori_loop(0, steps, full_step, 0)
+    begun = steps * HALVES + 1
+    pairs = (jnp.maximum(count - begun, 0) + 1) // 2
+
+    @pl.when(pairs >= 2)
+    def _():
+        step(begun, 4)
+
+    @pl.when(pairs % 2 == 1)
+    def _():
+        step(begun + pairs // 2 * 4, 2)
+
+    diagonal = lax.broadcasted_iota(jnp.int32, (128, 128), 0) == lane
+
+    def in_rows(array, begin):
+        rows = []
+        for r in range(0, BLOCKS * ROWS, 128):
+            square = jnp.where(diagonal, array[r : r + 128, begin : begin + 128], 0.0)
+            rows.append(jnp.sum(square, axis=0, keepdims=True))
+        return jnp.concatenate(rows, 0)
+
+    sums[...] = in_rows(acc, 128)
+    wrong = jnp.where(sums[...] < SUM_LIMIT, 0.0, 1.0)
 
     @pl.when(jnp.max(wrong) > 0.5)
     def _():
@@ -168,39 +193,40 @@
             return carry
 
         lax.fori_loop(0, BLOCKS * ROWS // SUB, redo, 0)
-
-    diagonal = lax.broadcasted_iota(jnp.int32, (128, 128), 0) == lane
+        sums[...] = in_rows(acc, 128)
+
+    notes = []
+    for value in (in_rows(top, 0), sums[...]):
+        high = value.astype(BF16)
+        rest = value - high.astype(F32)
+        middle = rest.astype(BF16)
+        notes += [high, middle, (rest - middle.astype(F32)).astype(BF16)]
+    blank = jnp.zeros((NOTE - 128 - 6, 128), BF16)
     for b in range(BLOCKS):
         for quarter in range(4):
-            r = b * ROWS + quarter * 128
-            total = acc[r : r + 128, 128:]
-            out[place[b], quarter, 0:128] = (acc[r : r + 128, 0:128] / total).astype(BF16)
-            lse = top[r : r + 128] + jnp.log2(total)
-            lse = jnp.sum(jnp.where(diagonal, lse, 0.0), axis=0, keepdims=True)
-            high = lse.astype(BF16).astype(F32)
-            middle = (lse - high).astype(BF16).astype(F32)
-            low = lse - high - middle
-            row = lax.broadcasted_iota(jnp.int32, (16, 128), 0)
-            note = jnp.where(row == 0, high, jnp.where(row == 1, middle, jnp.where(row == 2, low, 0.0)))
-            out[place[b], quarter, 128:NOTE] = note.astype(BF16)
+            n = b * 4 + quarter
+            out[place[b], quarter, 0:128] = acc[n * 128 : n * 128 + 128, 0:128].astype(BF16)
+            rows = [note[n : n + 1] for note in notes]
+            out[place[b], quarter, 128:NOTE] = jnp.concatenate([*rows, blank], 0)
 
 
 def attend(scalars, queries, kv, head):
     return pl.pallas_call(
         functools.partial(attend_kernel, head=head),
         out_shape=jax.ShapeDtypeStruct((BLOCKS, 4, NOTE, 128), BF16),
-        in_specs=[pl.BlockSpec(memory_space=pltpu.SMEM)] * 4
-        + [pl.BlockSpec(memory_space=pl.ANY)] * (BLOCKS + 5),
+        in_specs=[pl.BlockSpec(memory_space=pltpu.SMEM)] * 3
+        + [pl.BlockSpec(memory_space=pltpu.HBM)] * 8,
         out_specs=pl.BlockSpec(memory_space=pltpu.VMEM),
         scratch_shapes=[
             pltpu.VMEM((BLOCKS, SPAN, GROUP, 128), BF16),
-            pltpu.VMEM((4, 2, KEYS, 128), BF16),
+            pltpu.VMEM((4, 2, PACKED, 128), BF16),
             pltpu.VMEM((BLOCKS * ROWS, 256), F32),
             pltpu.VMEM((BLOCKS * ROWS, 128), F32),
             pltpu.VMEM((2, 128, 128), BF16),
-            pltpu.SemaphoreType.DMA((BLOCKS + 5,)),
+            pltpu.VMEM((BLOCKS * 4, 128), F32),
+            pltpu.SemaphoreType.DMA((BLOCKS + 4,)),
         ],
-        compiler_params=pltpu.CompilerParams(vmem_limit_bytes=40 << 20),
+        compiler_params=pltpu.CompilerParams(vmem_limit_bytes=62 << 20),
         cost_estimate=pl.CostEstimate(
             flops=2 * 2 * BLOCKS * ROWS * 4 * KEYS * 256,
             bytes_accessed=8 << 20,
@@ -214,13 +240,14 @@
     eye = lax.broadcasted_iota(jnp.int32, (128, 128), 0) == lax.broadcasted_iota(jnp.int32, (128, 128), 1)
     for source in range(4):
         for head, ref in enumerate((first, second)):
-            lse = []
+            tops, sums = [], []
             for b in range(BLOCKS):
                 note = ref[b * 4 + source, 128:NOTE].astype(F32)
-                lse.append(note[0:1] + note[1:2] + note[2:3])
-            largest = functools.reduce(jnp.maximum, lse)
-            weights = [jnp.exp2(x - largest) for x in lse]
-            total = functools.reduce(jnp.add, weights)
+                tops.append(note[0:1] + note[1:2] + note[2:3])
+                sums.append(note[3:4] + note[4:5] + note[5:6])
+            largest = functools.reduce(jnp.maximum, tops)
+            weights = [jnp.exp2(t - largest) for t in tops]
+            total = functools.reduce(jnp.add, [w * s for w, s in zip(weights, sums)])
             left, right = [], []
             for b in range(BLOCKS):
                 weight = jnp.broadcast_to(weights[b] / total, (128, 128))
@@ -253,29 +280,36 @@
 def per_device(queries, cache_keys, cache_values, new_keys, new_values, lengths, span_offset):
     x, z, y = lax.axis_index("x"), lax.axis_index("z"), lax.axis_index("y")
 
+    digit = lax.broadcasted_iota(jnp.int32, (16, 128), 0)
+    length = lengths[0]
+    tail = jnp.where(digit == 0, length // 16, jnp.where(digit == 1, length % 16, 0)).astype(BF16)
+
     def packed(head):
-        k = jnp.concatenate([cache_keys[:, head], new_keys[:, head]], 0)
-        v = jnp.concatenate([cache_values[:, head], new_values[:, head]], 0)
+        k = jnp.concatenate([cache_keys[:, head], new_keys[:, head], tail], 0)
+        v = jnp.concatenate([cache_values[:, head], new_values[:, head], tail], 0)
         return jnp.stack([k, v])
 
-    def gathered(own):
-        left, right = moved(own, "y", 1), moved(own, "y", -1)
-        return own, left, right, moved(left[0], "y", 1), moved(right[1], "y", -1)
-
-    all_lengths = lax.all_gather(lengths[0], "y")
     beside = moved(queries, "z", 1)
-    blocks, homes = [], []
-    for dz, block in enumerate((queries, beside)):
-        for dx in (0, 1, -1, 2):
-            blocks.append(moved(block, "x", -dx) if dx else block)
-            homes.append(((x + dx) % 4, (z + dz) % 2))
+    queries, beside, cache_keys, cache_values = lax.optimization_barrier(
+        (queries, beside, cache_keys, cache_values)
+    )
+    own = packed(0)
+    left, right, far = (moved(own, "y", distance) for distance in (1, -1, 2))
+    both = jnp.stack([queries, beside])
+    after, before = moved(both, "x", -1), moved(both, "x", 1)
+    both_too, after, before = lax.optimization_barrier((both, after, before))
+    blocks = (both, after, before, moved(both_too, "x", 2))
+    left, right, far, late_own = lax.optimization_barrier((left, right, far, packed(1)))
+    early = (own, left, right, far)
+    late = (late_own, *(moved(late_own, "y", distance) for distance in (1, -1, 2)))
+    kv = (early, late)
+    homes = [((x + dx) % 4, (z + dz) % 2) for dx in (0, 1, -1, 2) for dz in (0, 1)]
     place = jnp.stack([hx * 2 + hz for hx, hz in homes]).astype(jnp.int32)
     query_start = jnp.stack([(hx * 8 + hz * 4 + y) * SPAN for hx, hz in homes]).astype(jnp.int32) + span_offset
     shards = jnp.stack([y, (y - 1) % 4, (y + 1) % 4, (y + 2) % 4]).astype(jnp.int32)
     key_start = (x * 8 + z * 4 + shards) * SPAN
-    scalars = (all_lengths[shards], key_start, query_start, place)
-
-    kv = [gathered(packed(head)) for head in range(2)]
+    scalars = (key_start, query_start, place)
+
     partials = []
     for head in range(2):
         partial = attend(scalars, blocks, kv[head], head)

time: 441 us -> 518 us (1.17)
  the two profiles are of different devices: /device:TPU:9 before, /device:TPU:24 now
where the time goes in v2:
time: 518 us; the launch traced here: 524 us
  Pallas kernels  444 us (86%)
  waiting for transfers between devices  25.2 us (5%)
  blocking collectives  23.9 us (5%)
  starting transfers between devices  22.4 us (4%)
    pallas_call x2, Pallas kernels, attend(): pl.pallas_call(functools.partial(attend_kernel, head=head), out_shape=jax...  443 us
    ppermute x10, waiting for transfers between devices, moved(): lax.ppermute(block, axis, [(i, (i + distance) % size) for i in range(size)])  25.2 us
    all_to_all x1, blocking collectives, per_device(): lax.all_to_all(partial.reshape(BLOCKS * 4, NOTE, 128), ('x', 'z', 'head')...  23.9 us
    ppermute x10, starting transfers between devices, moved(): lax.ppermute(block, axis, [(i, (i + distance) % size) for i in range(size)])  17.2 us
  transfers between devices with their start and end apart: 11, of which 4 were waited for; matrix products, arithmetic and copies ran while one was open for 1% of the time, Pallas kernels for 84%

profile of v2, /device:TPU:24, one launch (start us, length us, event | category | flops | bytes accessed | tf_op | source)
XLA Modules:
  0.0 524.5 jit_solution(10928793344282223201)
XLA Ops:
  0.0 1.9 collective-permute-start
  2.6 0.8 fusion.5
  3.5 0.8 fusion.6
  4.4 4.0 collective-permute-done
  8.4 1.1 pad_maximum_fusion.6.refs_0_
  9.5 1.6 collective-permute-start.2
  11.1 1.7 collective-permute-start.1
  13.3 1.3 collective-permute-start.6
  14.6 3.2 collective-permute-start.4
  17.9 6.0 %collective-permute-done.2.refs_2_ = bf16[2,32,32,128]{3,2,1,0:T(8,128)(2,1)} collective-permute-done((bf16[2,32,32,128]{3,2,1,0:T(8,128)(2,1)S(1)}, bf16[2,32,32,128]{3,2,1,0:T(8,128)(2,1)}, u32[]{:S(2)}, u32[]{:S(2)}) %collective-permute-start.2) | collective-permute-done | bytes 524320 | tf_op jit(solution)/shard_map/ppermute | solution.py:277
  23.9 2.7 collective-permute-start.3
  26.6 0.6 fusion.4.key_start
  27.9 0.7 stack.118.place
  29.2 0.9 pad_maximum_fusion.5.refs_4_
  30.1 3.0 collective-permute-done.6.refs_7_
  33.1 12.1 %collective-permute-done.5.refs_6_ = bf16[2,1328,128]{2,1,0:T(8,128)(2,1)S(1)} collective-permute-done((bf16[2,1328,128]{2,1,0:T(8,128)(2,1)S(1)}, bf16[2,1328,128]{2,1,0:T(8,128)(2,1)S(1)}, u32[]{:S(2)}, u32[]{:S(2)}) %collective-permute-start.5) | collective-permute-done | bytes 679968 | tf_op jit(solution)/shard_map/ppermute | solution.py:277
  45.2 1.5 collective-permute-start.9
  46.8 3.2 collective-permute-start.7
  50.0 221.2 %attend.2 = bf16[8,4,144,128]{3,2,1,0:T(8,128)(2,1)} custom-call(s32[4]{0:T(128)} %fusion.4.key_start, s32[8]{0:T(128)} %broadcast_add_fusion.query_start, s32[8]{0:T(128)} %stack.118.place, bf16[2,32,32,128]{3,2,1,0:T(8,128)(2,1)} %copy-done.3, bf16[2,32,32,128]{3,2,1,0:T(8,128)(2,1)} %collective-permute-done.1.refs_1_, ...), custom_call_target="tpu_custom_call" | custom-call | flops 22011707392 | bytes 8388608 | tf_op jit(solution)/shard_map/attend/pallas_call | solution.py:214
  271.2 5.2 all-to-all-start
  276.4 0.8 copy-done.6
  277.3 221.3 %attend.3 = bf16[8,4,144,128]{3,2,1,0:T(8,128)(2,1)} custom-call(s32[4]{0:T(128)} %fusion.4.key_start, s32[8]{0:T(128)} %broadcast_add_fusion.query_start, s32[8]{0:T(128)} %stack.118.place, bf16[2,32,32,128]{3,2,1,0:T(8,128)(2,1)} %copy-done.3, bf16[2,32,32,128]{3,2,1,0:T(8,128)(2,1)} %collective-permute-done.1.refs_1_, ...), custom_call_target="tpu_custom_call" | custom-call | flops 22011707392 | bytes 8388608 | tf_op jit(solution)/shard_map/attend/pallas_call | solution.py:214
  498.6 23.9 %all_to_all.10.second = bf16[32,144,128]{2,1,0:T(8,128)(2,1)S(1)} all-to-all(bf16[32,144,128]{2,1,0:T(8,128)(2,1)} %bitcast.54), channel_id=1, replica_groups=mesh['x'=4,'z'=2,'y'=4,'head'=4] {'x','z','head'}, dimensions={0} | all-to-all | bytes 2359296 | tf_op jit(solution)/shard_map/all_to_all | solution.py:317
  522.5 2.0 merge.1
  (34 shorter events, 1.2 us)
Async XLA Ops:
  0.0 12.8 %copy-start.1 = (bf16[1280,2,128]{2,1,0:T(2,128)(2,1)S(1)}, bf16[1280,2,128]{2,1,0:T(2,128)(2,1)}, u32[]{:S(2)}) copy-start(bf16[1280,2,128]{2,1,0:T(2,128)(2,1)} %param.8) | copy-start | bytes 1966084
  0.0 8.4 %collective-permute-start = (bf16[32,32,128]{2,1,0:T(8,128)(2,1)}, bf16[32,32,128]{2,1,0:T(8,128)(2,1)S(1)}, u32[]{:S(2)}, u32[]{:S(2)}) collective-permute-start(bf16[32,32,128]{2,1,0:T(8,128)(2,1)} %param.7), channel_id=1, source_target_pairs={{0,16},{16,0},{1,17},{17,1},{2,18},{18,2},{3,19},{19,3},{4,20},{20... | collective-permute-start | bytes 786440 | tf_op jit(solution)/shard_map/ppermute | solution.py:277
  8.4 4.5 copy-start.2
  9.5 14.4 %copy-start.3 = (bf16[2,32,32,128]{3,2,1,0:T(8,128)(2,1)}, bf16[2,32,32,128]{3,2,1,0:T(8,128)(2,1)S(1)}, u32[]{:S(2)}) copy-start(bf16[2,32,32,128]{3,2,1,0:T(8,128)(2,1)S(1)} %pad_maximum_fusion.6.refs_0_) | copy-start | bytes 1572868
  9.5 14.4 %collective-permute-start.2 = (bf16[2,32,32,128]{3,2,1,0:T(8,128)(2,1)S(1)}, bf16[2,32,32,128]{3,2,1,0:T(8,128)(2,1)}, u32[]{:S(2)}, u32[]{:S(2)}) collective-permute-start(bf16[2,32,32,128]{3,2,1,0:T(8,128)(2,1)S(1)} %pad_maximum_fusion.6.refs_0_), channel_id=1, source_target_pairs={{0,32},{32,64},{64,96},{96,0},{1,33},{33,65},{65,97},{97,1},{2,34}... | collective-permute-start | bytes 1572872 | tf_op jit(solution)/shard_map/ppermute | solution.py:277
  11.1 12.8 %collective-permute-start.1 = (bf16[2,32,32,128]{3,2,1,0:T(8,128)(2,1)S(1)}, bf16[2,32,32,128]{3,2,1,0:T(8,128)(2,1)}, u32[]{:S(2)}, u32[]{:S(2)}) collective-permute-start(bf16[2,32,32,128]{3,2,1,0:T(8,128)(2,1)S(1)} %pad_maximum_fusion.6.refs_0_), channel_id=1, source_target_pairs={{0,96},{32,0},{64,32},{96,64},{1,97},{33,1},{65,33},{97,65},{2,98}... | collective-permute-start | bytes 1572872 | tf_op jit(solution)/shard_map/ppermute | solution.py:277
  13.3 36.7 %copy-start = (bf16[2,1328,128]{2,1,0:T(8,128)(2,1)}, bf16[2,1328,128]{2,1,0:T(8,128)(2,1)S(1)}, u32[]{:S(2)}) copy-start(bf16[2,1328,128]{2,1,0:T(8,128)(2,1)S(1)} %pad_maximum_fusion.4.refs_4_) | copy-start | bytes 2039812
  13.3 19.8 %collective-permute-start.6 = (bf16[2,1328,128]{2,1,0:T(8,128)(2,1)S(1)}, bf16[2,1328,128]{2,1,0:T(8,128)(2,1)S(1)}, u32[]{:S(2)}, u32[]{:S(2)}) collective-permute-start(bf16[2,1328,128]{2,1,0:T(8,128)(2,1)S(1)} %pad_maximum_fusion.4.refs_4_), channel_id=1, source_target_pairs={{0,8},{4,12},{8,0},{12,4},{1,9},{5,13},{9,1},{13,5},{2,10},{6,14},... | collective-permute-start | bytes 2039816 | tf_op jit(solution)/shard_map/ppermute | solution.py:277
  14.6 30.6 %collective-permute-start.5 = (bf16[2,1328,128]{2,1,0:T(8,128)(2,1)S(1)}, bf16[2,1328,128]{2,1,0:T(8,128)(2,1)S(1)}, u32[]{:S(2)}, u32[]{:S(2)}) collective-permute-start(bf16[2,1328,128]{2,1,0:T(8,128)(2,1)S(1)} %pad_maximum_fusion.4.refs_4_), channel_id=1, source_target_pairs={{0,12},{4,0},{8,4},{12,8},{1,13},{5,1},{9,5},{13,9},{2,14},{6,2},{... | collective-permute-start | bytes 2039816 | tf_op jit(solution)/shard_map/ppermute | solution.py:277
  14.6 30.6 %collective-permute-start.4 = (bf16[2,1328,128]{2,1,0:T(8,128)(2,1)S(1)}, bf16[2,1328,128]{2,1,0:T(8,128)(2,1)}, u32[]{:S(2)}, u32[]{:S(2)}) collective-permute-start(bf16[2,1328,128]{2,1,0:T(8,128)(2,1)S(1)} %pad_maximum_fusion.4.refs_4_), channel_id=1, source_target_pairs={{0,4},{4,8},{8,12},{12,0},{1,5},{5,9},{9,13},{13,1},{2,6},{6,10},{... | collective-permute-start | bytes 2039816 | tf_op jit(solution)/shard_map/ppermute | solution.py:277
  23.9 26.1 %collective-permute-start.3 = (bf16[2,32,32,128]{3,2,1,0:T(8,128)(2,1)S(1)}, bf16[2,32,32,128]{3,2,1,0:T(8,128)(2,1)}, u32[]{:S(2)}, u32[]{:S(2)}) collective-permute-start(bf16[2,32,32,128]{3,2,1,0:T(8,128)(2,1)S(1)} %pad_maximum_fusion.6.refs_0_), channel_id=1, source_target_pairs={{0,64},{32,96},{64,0},{96,32},{1,65},{33,97},{65,1},{97,33},{2,66}... | collective-permute-start | bytes 1572872 | tf_op jit(solution)/shard_map/ppermute | solution.py:277
  33.1 12.1 %copy-start.4 = (bf16[2,1328,128]{2,1,0:T(8,128)(2,1)}, bf16[2,1328,128]{2,1,0:T(8,128)(2,1)S(1)}, u32[]{:S(2)}) copy-start(bf16[2,1328,128]{2,1,0:T(8,128)(2,1)S(1)} %collective-permute-done.6.refs_7_) | copy-start | bytes 2039812
  45.2 1.5 copy-start.5
  45.2 231.2 %collective-permute-start.9 = (bf16[2,1328,128]{2,1,0:T(8,128)(2,1)}, bf16[2,1328,128]{2,1,0:T(8,128)(2,1)S(1)}, u32[]{:S(2)}, u32[]{:S(2)}) collective-permute-start(bf16[2,1328,128]{2,1,0:T(8,128)(2,1)} %pad_maximum_fusion.5.refs_4_), channel_id=1, source_target_pairs={{0,8},{4,12},{8,0},{12,4},{1,9},{5,13},{9,1},{13,5},{2,10},{6,14},... | collective-permute-start | bytes 2039816 | tf_op jit(solution)/shard_map/ppermute | solution.py:277
  46.7 229.7 %collective-permute-start.8 = (bf16[2,1328,128]{2,1,0:T(8,128)(2,1)}, bf16[2,1328,128]{2,1,0:T(8,128)(2,1)}, u32[]{:S(2)}, u32[]{:S(2)}) collective-permute-start(bf16[2,1328,128]{2,1,0:T(8,128)(2,1)} %pad_maximum_fusion.5.refs_4_), channel_id=1, source_target_pairs={{0,12},{4,0},{8,4},{12,8},{1,13},{5,1},{9,5},{13,9},{2,14},{6,2},{... | collective-permute-start | bytes 2039816 | tf_op jit(solution)/shard_map/ppermute | solution.py:277
  46.8 229.7 %collective-permute-start.7 = (bf16[2,1328,128]{2,1,0:T(8,128)(2,1)}, bf16[2,1328,128]{2,1,0:T(8,128)(2,1)}, u32[]{:S(2)}, u32[]{:S(2)}) collective-permute-start(bf16[2,1328,128]{2,1,0:T(8,128)(2,1)} %pad_maximum_fusion.5.refs_4_), channel_id=1, source_target_pairs={{0,4},{4,8},{8,12},{12,0},{1,5},{5,9},{9,13},{13,1},{2,6},{6,10},{... | collective-permute-start | bytes 2039816 | tf_op jit(solution)/shard_map/ppermute | solution.py:277
  271.2 227.4 %all-to-all-start = ((bf16[32,144,128]{2,1,0:T(8,128)(2,1)}), bf16[32,144,128]{2,1,0:T(8,128)(2,1)S(1)}, u32[]{:S(2)}, u32[]{:S(2)}) async-start(bf16[32,144,128]{2,1,0:T(8,128)(2,1)} %bitcast.53), calls=%async_computation | async-start | bytes 2359296 | tf_op jit(solution)/shard_map/all_to_all | solution.py:317
  276.4 0.9 copy-start.6
